TPU v7x, 128 devices: a whole 4x4x4 slice. The times are simulated.
128 devices in a mesh: user: 8 (over y, core), item: 16 (over x, z).
Axes of the slice: x: 4, y: 4, z: 4, core: 2. Of those that a mesh axis runs over, the one named last changes fastest.
Arguments:
- weights: bfloat16 [256, 192, 128, 128], P('user', 'item'), may hold values from 0.5 to 8
- ratings: bfloat16 [256, 192, 128, 128], P('user', 'item'), may hold values from -6 to 6
- tile_cols: int32 [256, 192], P('user', 'item'), may hold values from 0 to 31, as said below
- item_factors: bfloat16 [65536, 128], P('item'), may hold values from -1 to 1
- old_users: float32 [32768, 128], P('user'), may hold values from -6 to 6
Outputs:
- new_users: float32 [32768, 128], P(('user', 'item'))
Inputs may be any that keep to these rules, and one draw needn't show every extreme that they name: `tile_cols`: within each row, the 12 entries of one item block name distinct tile columns of that block.
All inputs are finite; a program needn't handle non-finite values.
Results may differ from a plain program's by a relative error of at most 0.0065.
Values may be sent and summed in bfloat16 or wider, within the bound.
A program may use at most 128 MiB of HBM per device.

v0:
```python
import jax
import jax.numpy as jnp
from jax import lax
from jax.sharding import PartitionSpec as P

ITERS = 3


ridge = 0.05


def shards(weights, ratings, tile_cols, item_factors, old_users):
    row_tiles, slots, tile, _ = weights.shape
    users_dev, width = old_users.shape
    col_tiles = item_factors.shape[0] // tile
    tiles_items = jnp.take(item_factors.reshape(col_tiles, tile, width), tile_cols, axis=0)

    def scores(rows):
        return jnp.einsum(
            "ruk,rsik->rsui",
            rows.reshape(row_tiles, tile, width),
            tiles_items,
            preferred_element_type=jnp.float32,
        )

    def spread(mixed):
        return jnp.einsum(
            "rsui,rsik->ruk", mixed, tiles_items, preferred_element_type=jnp.float32
        ).reshape(users_dev, width)

    share = users_dev // lax.axis_size("item")
    offset = lax.axis_index("item") * share

    def reduce_items(term):
        return lax.psum(term, "item")

    def norm_total(value):
        return lax.psum(value, "user")

    start = scores(old_users.astype(jnp.bfloat16))
    errors = (weights * (ratings.astype(jnp.float32) - start)).astype(jnp.bfloat16)
    residual = reduce_items(spread(errors)) - ridge * old_users
    solution = old_users
    direction = residual
    norm_now = norm_total(jnp.sum(residual * residual))
    for step in range(ITERS):
        rows = direction.astype(jnp.bfloat16)
        mixed = (weights * scores(rows)).astype(jnp.bfloat16)
        image = reduce_items(spread(mixed)) + ridge * direction
        alpha = norm_now / lax.psum(jnp.sum(direction * image), "user")
        solution = solution + alpha * direction
        residual = residual - alpha * image
        norm_next = norm_total(jnp.sum(residual * residual))
        direction = residual + norm_next / norm_now * direction
        norm_now = norm_next
    mine = lax.dynamic_slice_in_dim(solution, offset, share, 0)
    return lax.all_to_all(
        mine.astype(jnp.bfloat16), ("user", "item"), split_axis=0, concat_axis=0, tiled=True
    ).astype(mine.dtype)


def solution(mesh):
    placed = (
        P("user", "item", None, None),
        P("user", "item", None, None),
        P("user", "item"),
        P("item", None),
        P("user", None),
    )
    return jax.shard_map(
        shards, mesh=mesh, in_specs=placed, out_specs=P(("user", "item"), None), check_vma=False
    )
```

profile of v0, /device:TPU:1, one launch (start us, length us, event | category | flops | bytes accessed | tf_op | source)
XLA Modules:
  0.0 585.8 jit_solution(9111915613541201647)
XLA Ops:
  6.5 0.0 copy-start
  6.5 0.0 all-reduce.6.cloned.1.call-start
  6.5 0.8 compare_select_fusion
  7.3 0.7 compare_and_fusion
  8.0 0.1 copy.8
  8.1 0.1 reshape.48
  8.2 0.1 copy.7
  8.3 1.7 convert_element_type.44
  10.0 0.0 copy-done
  10.0 11.3 %gather_fusion = bf16[384,128,128]{2,1,0:T(8,128)(2,1)} fusion(bf16[32,128,128]{2,1,0:T(8,128)(2,1)S(1)} %bitcast.59, s32[1024]{0:T(1024)S(1)} %pad_clamp_fusion), kind=kCustom, calls=%fused_computation | custom fusion | bytes 25167360 | tf_op jit(solution)/shard_map/jit(_take)/gather | solution.py:16
  21.4 23.3 %fusion.16 = f32[32,128,128,1]{2,1,3,0:T(8,128)} fusion(bf16[32,12,128,128]{3,2,1,0:T(8,128)(2,1)} %param.5, bf16[32,12,128,128]{3,2,1,0:T(8,128)(2,1)} %param.6, bf16[32,128,128,1]{2,1,3,0:T(8,128)(2,1)S(1)} %bitcast.70, bf16[32,12,128,128]{3,2,1,0:T(8,128)(2,1)} %bitcast.60, pred[32,12]{1,0:T(8,128)(4,1)S(1)} %copy.7), kind=kOutput, calls=%fused_computation.16 | convolution fusion | flops 3265265664 | bytes 40894848 | tf_op jit(solution)/shard_map/rsui,rsik->ruk/dot_general | solution.py:27
  44.7 0.0 all-reduce.6.cloned.1.call-update
  44.7 0.0 all-reduce.8.cloned.1.call-start
  44.7 92.6 %all-reduce.6.cloned.1.call-done = f32[4096,128]{1,0:T(8,128)} async-done(((f32[4096,128]{1,0:T(8,128)}), f32[4096,128]{1,0:T(8,128)}) %all-reduce.6.cloned.1.call-update) | async-done | bytes 2097168 | tf_op jit(solution)/shard_map/psum | solution.py:35
  137.4 2.5 fusion.41
  139.9 19.0 %fusion.12 = f32[32,128,128,1]{2,1,3,0:T(8,128)} fusion(bf16[32,12,128,128]{3,2,1,0:T(8,128)(2,1)} %param.5, bf16[32,128,128,1]{2,1,3,0:T(8,128)(2,1)S(1)} %bitcast.69, bf16[32,12,128,128]{3,2,1,0:T(8,128)(2,1)} %bitcast.61, pred[32,12]{1,0:T(8,128)(4,1)S(1)} %copy.7), kind=kOutput, calls=%fused_computation.14 | convolution fusion | flops 3252682752 | bytes 28311936 | tf_op jit(solution)/shard_map/rsui,rsik->ruk/dot_general | solution.py:27
  158.9 0.0 all-reduce.8.cloned.1.call-update
  158.9 0.0 all-reduce.10.cloned.1.call-start
  159.0 89.8 %all-reduce.8.cloned.1.call-done = f32[4096,128]{1,0:T(8,128)} async-done(((f32[4096,128]{1,0:T(8,128)}), f32[4096,128]{1,0:T(8,128)}) %all-reduce.8.cloned.1.call-update) | async-done | bytes 2097168 | tf_op jit(solution)/shard_map/psum | solution.py:35
  248.8 2.8 multiply_reduce_fusion.4
  251.6 14.1 %all-reduce = (f32[]{:T(128)}, f32[]{:T(128)}) all-reduce(f32[]{:T(128)} %get-tuple-element.6, f32[]{:T(128)} %get-tuple-element.5), channel_id=1, replica_groups=mesh['user'=8,'item'=16] {'user'}, use_global_device_ids=true, to_apply=%region_2.3 | all-reduce | flops 2 | bytes 16 | tf_op jit(solution)/shard_map/psum | solution.py:38
  267.0 4.0 multiply_reduce_fusion.3
  271.0 14.3 %psum.74 = f32[]{:T(128)} all-reduce(f32[]{:T(128)} %get-tuple-element.13), channel_id=1, replica_groups=mesh['user'=8,'item'=16] {'user'}, use_global_device_ids=true, to_apply=%region_7.8 | all-reduce | flops 1 | bytes 8 | tf_op jit(solution)/shard_map/psum | solution.py:38
  286.6 3.2 fusion.40
  289.8 19.0 %fusion.8 = f32[32,128,128,1]{2,1,3,0:T(8,128)} fusion(bf16[32,12,128,128]{3,2,1,0:T(8,128)(2,1)} %param.5, bf16[32,128,128,1]{2,1,3,0:T(8,128)(2,1)S(1)} %bitcast.71, bf16[32,12,128,128]{3,2,1,0:T(8,128)(2,1)} %bitcast.62, pred[32,12]{1,0:T(8,128)(4,1)S(1)} %copy.7), kind=kOutput, calls=%fused_computation.12 | convolution fusion | flops 3252682752 | bytes 28311936 | tf_op jit(solution)/shard_map/rsui,rsik->ruk/dot_general | solution.py:27
  308.8 0.0 all-reduce.10.cloned.1.call-update
  308.8 0.0 all-reduce.12.cloned.1.call-start
  308.8 85.9 %all-reduce.10.cloned.1.call-done = f32[4096,128]{1,0:T(8,128)} async-done(((f32[4096,128]{1,0:T(8,128)}), f32[4096,128]{1,0:T(8,128)}) %all-reduce.10.cloned.1.call-update) | async-done | bytes 2097168 | tf_op jit(solution)/shard_map/psum | solution.py:35
  394.7 3.4 multiply_reduce_fusion.2
  398.1 14.1 %psum.76 = f32[]{:T(128)} all-reduce(f32[]{:T(128)} %multiply_reduce_fusion.2), channel_id=1, replica_groups=mesh['user'=8,'item'=16] {'user'}, use_global_device_ids=true, to_apply=%region_10.11 | all-reduce | flops 1 | bytes 8 | tf_op jit(solution)/shard_map/psum | solution.py:50
  413.6 4.1 multiply_reduce_fusion.1
  417.6 14.2 %psum.77 = f32[]{:T(128)} all-reduce(f32[]{:T(128)} %multiply_reduce_fusion.1), channel_id=1, replica_groups=mesh['user'=8,'item'=16] {'user'}, use_global_device_ids=true, to_apply=%region_12.13 | all-reduce | flops 1 | bytes 8 | tf_op jit(solution)/shard_map/psum | solution.py:38
  433.2 5.0 fusion.39
  438.2 0.0 copy-start.1
  438.2 19.3 %fusion.4 = f32[32,128,128,1]{2,1,3,0:T(8,128)} fusion(bf16[32,12,128,128]{3,2,1,0:T(8,128)(2,1)} %param.5, bf16[32,128,128,1]{2,1,3,0:T(8,128)(2,1)} %bitcast.68, bf16[32,12,128,128]{3,2,1,0:T(8,128)(2,1)} %bitcast.63, pred[32,12]{1,0:T(8,128)(4,1)S(1)} %copy.7), kind=kOutput, calls=%fused_computation.10 | convolution fusion | flops 3252682752 | bytes 28311936 | tf_op jit(solution)/shard_map/rsui,rsik->ruk/dot_general | solution.py:27
  457.5 0.0 all-reduce.12.cloned.1.call-update
  457.5 86.0 %all-reduce.12.cloned.1.call-done = f32[4096,128]{1,0:T(8,128)} async-done(((f32[4096,128]{1,0:T(8,128)}), f32[4096,128]{1,0:T(8,128)}) %all-reduce.12.cloned.1.call-update) | async-done | bytes 2097168 | tf_op jit(solution)/shard_map/psum | solution.py:35
  543.5 3.4 multiply_reduce_fusion
  546.9 14.1 %psum.79 = f32[]{:T(128)} all-reduce(f32[]{:T(128)} %multiply_reduce_fusion), channel_id=1, replica_groups=mesh['user'=8,'item'=16] {'user'}, use_global_device_ids=true, to_apply=%region_15.16 | all-reduce | flops 1 | bytes 8 | tf_op jit(solution)/shard_map/psum | solution.py:50
  562.3 1.1 fusion.29
  563.4 15.2 %all_to_all.9 = bf16[128,2,128]{2,1,0:T(2,128)(2,1)S(1)} all-to-all(bf16[128,2,128]{2,1,0:T(2,128)(2,1)S(1)} %bitcast.72), channel_id=1, replica_groups=mesh['user'=8,'item'=16] {'user','item'}, dimensions={0} | all-to-all | bytes 131072 | tf_op jit(solution)/shard_map/all_to_all | solution.py:57
  578.6 0.7 convert.1
  579.3 0.0 copy-done.1
  (1 shorter events, 0.0 us)
Async XLA Ops:
  6.5 3.5 copy-start
  6.5 130.8 %all-reduce.6.cloned.1.call-start = ((), (), s32[]{:S(2)}) async-start(), calls=%async_computation.1 | async-start | bytes 4194304 | tf_op jit(solution)/shard_map/psum | solution.py:35
  44.7 204.1 %all-reduce.8.cloned.1.call-start = ((), (), s32[]{:S(2)}) async-start(), calls=%async_computation.2 | async-start | bytes 4194304 | tf_op jit(solution)/shard_map/psum | solution.py:35
  158.9 235.8 %all-reduce.10.cloned.1.call-start = ((), (), s32[]{:S(2)}) async-start(), calls=%async_computation.3 | async-start | bytes 4194304 | tf_op jit(solution)/shard_map/psum | solution.py:35
  308.8 234.7 %all-reduce.12.cloned.1.call-start = ((), (), s32[]{:S(2)}) async-start(), calls=%async_computation.4 | async-start | bytes 4194304 | tf_op jit(solution)/shard_map/psum | solution.py:35
  438.2 141.1 %copy-start.1 = (bf16[4096,128]{1,0:T(8,128)(2,1)S(1)}, bf16[4096,128]{1,0:T(8,128)(2,1)}, u32[]{:S(2)}) copy-start(bf16[4096,128]{1,0:T(8,128)(2,1)} %param.8) | copy-start | bytes 3145732
Sparse Core Ops, SparseCore 0:
  44.8 92.5 all-reduce.5
  159.1 89.6 all-reduce.7
  308.9 85.7 all-reduce.9
  457.6 85.8 all-reduce.11
where the time goes:
time: 586 us
  waiting for transfers between devices  354 us (60%)
  blocking collectives  86.2 us (15%)
  matrix products  80.6 us (14%)
  other arithmetic  33.4 us (6%)
  between operations  19.6 us (3%)
  local copies, waits for them, and re-layouts  11.6 us (2%)
    psum x4, waiting for transfers between devices, reduce_items(): return lax.psum(term, 'item')  354 us
    dot_general x4, matrix products, spread(): jnp.einsum('rsui,rsik->ruk', mixed, tiles_items, preferred_element_type=j...  80.6 us
    psum x3, blocking collectives, norm_total(): return lax.psum(value, 'user')  42.7 us
    psum x2, blocking collectives, shards(): alpha = norm_now / lax.psum(jnp.sum(direction * image), 'user')  28.3 us
    all_to_all x1, blocking collectives, shards(): lax.all_to_all(mine.astype(jnp.bfloat16), ('user', 'item'), split_axis=0,...  15.2 us
  transfers between devices with their start and end apart: 4, of which 4 were waited for; matrix products, arithmetic and copies ran while one was open for 0% of the time, Pallas kernels for 0%

commit v1 on v0

v1 whole, which is shorter than its diff:
```python
import jax
import jax.numpy as jnp
from jax import lax
from jax.experimental import pallas as pl
from jax.experimental.pallas import tpu as pltpu
from jax.sharding import PartitionSpec as P

MESH = pl.DeviceIdType.MESH
BF = jnp.bfloat16
F32 = jnp.float32
RIDGE = 0.05
T = 128
SLOTS = 12
NI = 16
NU = 8
SH = 256


def near(a):
    return a + a // 2 - 2 * (a // 3)


def div(a, b):
    ok = b != 0.0
    return jnp.where(ok, a / jnp.where(ok, b, 1.0), 0.0)


def lanes(a):
    return jnp.sum(a, axis=0, keepdims=True)


def total(a):
    return jnp.broadcast_to(jnp.sum(a, axis=1, keepdims=True), (1, T))


def kernel(
    cols, w_hbm, r_hbm, i_hbm, x_hbm, out,
    w, rt, it, tt, x0, q0, q1, part, got, vec, wide, v0, y0, t1, y1, t2, acc, sj, og,
    us_in, us_out, ps_in, ps_out, xd_out, xd_in,
    w_sem, r_sem, i_sem, rs_s, rs_r, ag_s, ag_r, us_s, us_r, ps_s, ps_r, xd_s, xd_r,
):
    u = lax.axis_index("user")
    i = lax.axis_index("item")
    x, z = i // 4, lax.rem(i, 4)

    def shard(k):
        return lax.rem(x + near(k // 4), 4) * 4 + lax.rem(z + near(lax.rem(k, 4)), 4)

    def mate(k):
        return lax.rem(u + k, NU)

    bar = pltpu.get_barrier_semaphore()

    def greet_plane(k, c):
        pl.semaphore_signal(bar, inc=1, device_id=(u, shard(k)), device_id_type=MESH)
        return c

    def greet_user(k, c):
        pl.semaphore_signal(bar, inc=1, device_id=(mate(k), i), device_id_type=MESH)
        return c

    load_i = pltpu.make_async_copy(i_hbm, it, i_sem.at[0])
    load_x = pltpu.make_async_copy(x_hbm, x0, i_sem.at[1])

    def load_w(j):
        rows = pl.ds(2 * j, 2)
        return pltpu.make_async_copy(w_hbm.at[rows], w.at[rows], w_sem.at[j])

    def load_r(j):
        rows = pl.ds(2 * j, 2)
        return pltpu.make_async_copy(r_hbm.at[rows], rt.at[rows], r_sem.at[j])

    load_i.start()
    load_x.start()

    def start_loads(k, c):
        j = shard(15 - k)
        load_w(j).start()
        load_r(j).start()
        return c

    lax.fori_loop(0, NI, start_loads, 0)
    lax.fori_loop(1, NI, greet_plane, 0)
    lax.fori_loop(1, NU, greet_user, 0)

    load_i.wait()

    def turn(c, carry):
        tt[c] = it[c].T
        return carry

    lax.fori_loop(0, 32, turn, 0)
    load_x.wait()

    def rs_copy(n, j):
        return pltpu.make_async_remote_copy(
            src_ref=part.at[n, j], dst_ref=got.at[n, i], send_sem=rs_s.at[n, j], recv_sem=rs_r.at[n, i],
            device_id=(u, j), device_id_type=MESH)

    def rs_arrival(n, j):
        return pltpu.make_async_remote_copy(
            src_ref=part.at[n, j], dst_ref=got.at[n, j], send_sem=rs_s.at[n, j], recv_sem=rs_r.at[n, j],
            device_id=(u, j), device_id_type=MESH)

    def ag_copy(n, j):
        return pltpu.make_async_remote_copy(
            src_ref=vec.at[n, i], dst_ref=vec.at[n, i], send_sem=ag_s.at[n, j], recv_sem=ag_r.at[n, i],
            device_id=(u, j), device_id_type=MESH)

    def ag_arrival(n, j):
        return pltpu.make_async_remote_copy(
            src_ref=vec.at[n, i], dst_ref=vec.at[n, j], send_sem=ag_s.at[n, j], recv_sem=ag_r.at[n, j],
            device_id=(u, j), device_id_type=MESH)

    def us_copy(m, o, slot):
        return pltpu.make_async_remote_copy(
            src_ref=us_out.at[m], dst_ref=us_in.at[m, slot], send_sem=us_s.at[m, o], recv_sem=us_r.at[m, slot],
            device_id=(o, i), device_id_type=MESH)

    def ps_copy(m, j, slot):
        return pltpu.make_async_remote_copy(
            src_ref=ps_out.at[m], dst_ref=ps_in.at[m, slot], send_sem=ps_s.at[m, j], recv_sem=ps_r.at[m, slot],
            device_id=(u, j), device_id_type=MESH)

    def xd_copy(o, slot):
        return pltpu.make_async_remote_copy(
            src_ref=xd_out.at[pl.ds(pl.multiple_of(o * 64, 64), 64)], dst_ref=xd_in.at[slot],
            send_sem=xd_s.at[o], recv_sem=xd_r.at[slot], device_id=(o, i), device_id_type=MESH)

    def each(lo, hi, fn):
        def body(k, c):
            fn(k)
            return c
        lax.fori_loop(lo, hi, body, 0)

    def score_pair(d, r, p):
        t = jnp.concatenate([tt[cols[r, 2 * p]], tt[cols[r, 2 * p + 1]]], axis=1)
        return jnp.dot(d, t, preferred_element_type=F32)

    def weight_pair(ref, r, p):
        return jnp.concatenate([ref[r, 2 * p], ref[r, 2 * p + 1]], axis=1).astype(F32)

    def rows_of(n, j, h):
        if n == 0:
            return x0[pl.ds(pl.multiple_of(j * SH + h * T, T), T), :].astype(BF)
        d = vec[n - 1, j, h * T:(h + 1) * T, :]
        wide[n - 1, pl.ds(pl.multiple_of(j * SH + h * T, T), T), :] = d.astype(F32)
        return d

    def scores(n, j, q):
        for h in range(2):
            r = 2 * j + h
            d = rows_of(n, j, h)
            for p in range(SLOTS // 2):
                s = score_pair(d, r, p)
                if n == 0:
                    s = weight_pair(rt, r, p) - s
                q[h * T:(h + 1) * T, 2 * T * p:2 * T * (p + 1)] = (weight_pair(w, r, p) * s).astype(BF)

    def spread(n, j, q):
        for h in range(2):
            r = 2 * j + h
            items = jnp.concatenate([it[cols[r, b]] for b in range(SLOTS)], axis=0)
            part[n, j, h * T:(h + 1) * T, :] = jnp.dot(
                q[h * T:(h + 1) * T, :], items, preferred_element_type=F32).astype(BF)

    def run_pass(n):
        first = n == 0

        def at(k):
            return shard(15 - k) if first else shard(k)

        def ready(k):
            j = at(k)
            if first:
                load_w(j).wait()
                load_r(j).wait()
            else:
                ag_arrival(n - 1, j).wait_recv()

        if first:
            ready(0)
        scores(n, at(0), q0)

        def two(kk, c):
            a, b = at(2 * kk), at(2 * kk + 1)
            ready(2 * kk + 1)
            spread(n, a, q0)
            scores(n, b, q1)
            if first:
                @pl.when(kk == 0)
                def _():
                    pl.semaphore_wait(bar, NI - 1 + NU - 1)
                rs_copy(n, a).start()
            else:
                @pl.when(kk > 0)
                def _():
                    rs_copy(n, a).start()
            ready(2 * kk + 2)
            spread(n, b, q1)
            scores(n, at(2 * kk + 2), q0)
            rs_copy(n, b).start()
            return c

        lax.fori_loop(0, 7, two, 0)
        a, b = at(14), at(15)
        ready(15)
        spread(n, a, q0)
        scores(n, b, q1)
        rs_copy(n, a).start()
        spread(n, b, q1)
        if not first:
            rs_copy(n, b).start()

    def collect(n):
        acc[...] = part[n, i].astype(F32)

        def add(k):
            j = shard(k)
            rs_arrival(n, j).wait_recv()
            acc[...] += got[n, j].astype(F32)

        each(1, NI, add)
        return acc[...]

    def publish(n, value):
        vec[n, i] = value.astype(BF)
        each(1, NI, lambda k: ag_copy(n, shard(k)).start())

    def user_send(m):
        each(1, NU, lambda k: us_copy(m, mate(k), u).start())

    def user_sum(m):
        us_in[m, u] = us_out[m]

        def wait(k):
            us_copy(m, mate(k), mate(k)).wait_recv()

        each(1, NU, wait)
        return jnp.sum(us_in[m], axis=0)

    def plane_send(m):
        each(1, NI, lambda k: ps_copy(m, shard(k), i).start())

    def plane_sum(m):
        ps_in[m, i] = ps_out[m]

        def wait(k):
            ps_copy(m, shard(k), shard(k)).wait_recv()

        each(1, NI, wait)
        return jnp.sum(ps_in[m, :, 0:8, :], axis=0)

    def pick(tile, m):
        return total(tile[m:m + 1, :])

    zero = jnp.zeros((1, T), F32)
    mine = pl.ds(pl.multiple_of(i * SH, SH), SH)

    run_pass(0)
    v0[...] = collect(0) - RIDGE * x0[mine, :]
    publish(0, v0[...])
    vv = lanes(v0[...] * v0[...])

    run_pass(1)
    y0[...] = collect(1) + RIDGE * v0[...]
    vy = lanes(v0[...] * y0[...])
    inv_alpha = div(total(vy), total(vv))
    alpha = div(total(vv), total(vy))
    t1[...] = v0[...] - alpha * y0[...]
    publish(1, t1[...])
    us_out[0] = jnp.concatenate([vv, vy, zero, zero, zero, zero, zero, zero], axis=0)
    user_send(0)

    run_pass(2)
    ps_out[0, 0:8, :] = user_sum(0)
    ps_out[0, 8:16, :] = jnp.zeros((8, T), F32)
    plane_send(0)
    y1[...] = collect(2) + RIDGE * t1[...]
    tt1 = lanes(t1[...] * t1[...])
    beta_own = div(total(tt1), total(vv))
    vy1 = lanes(v0[...] * y1[...])
    ty0 = lanes(t1[...] * y0[...])
    ty1 = lanes(t1[...] * y1[...])
    dad_own = total(ty1 + beta_own * (ty0 + vy1) + beta_own * beta_own * vy)
    alpha1 = div(total(tt1), dad_own)
    inv_alpha1 = div(dad_own, total(tt1))
    t2[...] = t1[...] - alpha1 * (y1[...] + beta_own * y0[...])
    publish(2, t2[...])
    og[...] = jnp.concatenate([
        vy, ty0, ty1, lanes(t2[...] * y0[...]), lanes(t2[...] * y1[...]), lanes(t2[...] * t2[...]), zero, zero], axis=0)

    sums0 = plane_sum(0)
    rr0, vy_all = pick(sums0, 0), pick(sums0, 1)
    a0 = rr0 / vy_all
    rho = a0 * inv_alpha
    r1 = v0[...] - a0 * y0[...]
    z1 = rho * y1[...] + (1.0 - rho) * y0[...]
    us_out[1] = jnp.concatenate([
        lanes(r1 * r1), lanes(r1 * z1), lanes(r1 * y0[...]), lanes(v0[...] * z1), lanes(z1 * z1),
        lanes(z1 * y0[...]), lanes(y0[...] * y0[...]), zero], axis=0)
    user_send(1)
    ps_out[1, 8:16, :] = jnp.concatenate([inv_alpha, inv_alpha1, beta_own, zero, zero, zero, zero, zero], axis=0)

    def squares(k):
        j = shard(k)
        out_sum = jnp.zeros((8, T), F32)
        for h in range(2):
            r = 2 * j + h
            d = rows_of(3, j, h)
            part_sum = jnp.zeros((T, 2 * T), F32)
            for p in range(SLOTS // 2):
                s = score_pair(d, r, p)
                part_sum += weight_pair(w, r, p) * s * s
            out_sum += jnp.sum((part_sum[:, :T] + part_sum[:, T:]).reshape(T // 8, 8, T), axis=0)
        sj[j] = out_sum

    def arrive_squares(k):
        ag_arrival(2, shard(k)).wait_recv()
        squares(k)

    squares(0)
    each(1, 8, arrive_squares)
    ps_out[1, 0:8, :] = user_sum(1)
    plane_send(1)
    each(8, NI, arrive_squares)

    sums1 = plane_sum(1)
    rr1, r1z1, r1y0, v0z1, z1z1, z1y0, y0y0 = [pick(sums1, m) for m in range(7)]
    b0 = rr1 / rr0
    a1 = rr1 / (r1z1 + b0 * (r1y0 + v0z1) + b0 * b0 * vy_all)
    rr2 = rr1 - 2.0 * a1 * (r1z1 + b0 * r1y0) + a1 * a1 * (z1z1 + 2.0 * b0 * z1y0 + b0 * b0 * y0y0)
    b1 = rr2 / rr1

    def coefficients(inv_a, inv_a1, beta):
        rho = a0 * inv_a
        h = a1 * (rho * beta - 1.0 + rho - b0) * inv_a
        e0 = (1.0 - rho + h) + b1 * (1.0 - rho + b0)
        e1 = rho - a1 * rho * inv_a1 - h + b1 * rho
        e2 = a1 * rho * inv_a1
        return a0 + a1 * (1.0 - rho + b0), a1 * rho, e0, e1, e2

    _, _, e0, e1, e2 = coefficients(inv_alpha, inv_alpha1, beta_own)
    g = og[...]
    own = (e0 * e0 * g[0:1] + 2.0 * e0 * e1 * g[1:2] + e1 * e1 * g[2:3] + 2.0 * e0 * e2 * g[3:4]
           + 2.0 * e1 * e2 * g[4:5] + e2 * e2 * RIDGE * g[5:6])

    def weigh(p, tot):
        _, _, _, _, e2 = coefficients(ps_in[1, p, 8:9, :], ps_in[1, p, 9:10, :], ps_in[1, p, 10:11, :])
        return tot + e2 * e2 * lanes(sj[p])

    us_out[2] = jnp.concatenate([lax.fori_loop(0, NI, weigh, own), zero, zero, zero, zero, zero, zero, zero], axis=0)
    user_send(2)

    def choose(p):
        f0, f1, e0, e1, e2 = coefficients(ps_in[1, p, 8:9, :], ps_in[1, p, 9:10, :], ps_in[1, p, 10:11, :])
        for e in range(2):
            rows = pl.ds(p * SH + 2 * i + e, NU, stride=32)
            a, b, c = wide[0, rows, :], wide[1, rows, :], wide[2, rows, :]
            xd_out[pl.ds(2 * p + e, NU, stride=64), :] = x0[rows, :] + f0 * a + f1 * b
            xd_out[pl.ds(32 + 2 * p + e, NU, stride=64), :] = e0 * a + e1 * b + e2 * c

    each(0, NI, choose)
    each(1, NU, lambda k: xd_copy(mate(k), u).start())

    ps_out[2, 0:8, :] = user_sum(2)
    ps_out[2, 8:16, :] = jnp.zeros((8, T), F32)
    plane_send(2)
    xd_in[u] = xd_out[pl.ds(pl.multiple_of(u * 64, 64), 64), :]
    each(1, NU, lambda k: xd_copy(mate(k), mate(k)).wait_recv())
    a2 = rr2 / pick(plane_sum(2), 0)
    for o in range(NU):
        out[o * 32:(o + 1) * 32, :] = xd_in[o, 0:32, :] + a2 * xd_in[o, 32:64, :]

    def sent_plane(k):
        j = shard(k)
        for n in range(3):
            rs_copy(n, j).wait_send()
            ag_copy(n, j).wait_send()
            ps_copy(n, j, i).wait_send()

    def sent_user(k):
        o = mate(k)
        for m in range(3):
            us_copy(m, o, u).wait_send()
        xd_copy(o, u).wait_send()

    each(1, NI, sent_plane)
    each(1, NU, sent_user)


def shards(weights, ratings, tile_cols, item_factors, old_users):
    vmem = pltpu.VMEM
    dma = pltpu.SemaphoreType.DMA
    any_space = pl.BlockSpec(memory_space=pl.ANY)
    return pl.pallas_call(
        kernel,
        out_shape=jax.ShapeDtypeStruct((SH, T), F32),
        in_specs=[pl.BlockSpec(memory_space=pltpu.SMEM), any_space, any_space, any_space, any_space],
        out_specs=pl.BlockSpec(memory_space=vmem),
        scratch_shapes=[
            vmem((32, SLOTS, T, T), BF), vmem((32, SLOTS, T, T), BF),
            vmem((32, T, T), BF), vmem((32, T, T), BF), vmem((4096, T), F32),
            vmem((SH, SLOTS * T), BF), vmem((SH, SLOTS * T), BF),
            vmem((3, NI, SH, T), BF), vmem((3, NI, SH, T), BF), vmem((3, NI, SH, T), BF), vmem((3, 4096, T), F32),
            vmem((SH, T), F32), vmem((SH, T), F32), vmem((SH, T), F32), vmem((SH, T), F32), vmem((SH, T), F32), vmem((SH, T), F32),
            vmem((NI, 8, T), F32), vmem((8, T), F32),
            vmem((3, NU, 8, T), F32), vmem((3, 8, T), F32), vmem((3, NI, 16, T), F32), vmem((3, 16, T), F32),
            vmem((NU * 64, T), F32), vmem((NU, 64, T), F32),
            dma((NI,)), dma((NI,)), dma((2,)),
            dma((3, NI)), dma((3, NI)), dma((3, NI)), dma((3, NI)),
            dma((3, NU)), dma((3, NU)), dma((3, NI)), dma((3, NI)), dma((NU,)), dma((NU,)),
        ],
        compiler_params=pltpu.CompilerParams(
            collective_id=0, has_side_effects=True, vmem_limit_bytes=56 * 2 ** 20),
    )(tile_cols, weights, ratings, item_factors.reshape(32, T, T), old_users)


def solution(mesh):
    placed = (
        P("user", "item", None, None),
        P("user", "item", None, None),
        P("user", "item"),
        P("item", None),
        P("user", None),
    )
    return jax.shard_map(
        shards, mesh=mesh, in_specs=placed, out_specs=P(("user", "item"), None), check_vma=False
    )
```

time: 586 us -> 131 us (0.22)
  waiting for transfers between devices: 354 us -> 0 us
  Pallas kernels: 0 us -> 127 us
  blocking collectives: 86.2 us -> 0 us
  matrix products: 80.6 us -> 0 us
  other arithmetic: 33.4 us -> 0 us
  between operations: 19.6 us -> 0.01 us
  local copies, waits for them, and re-layouts: 11.6 us -> 2.95 us
    psum x4 -> x0, waiting for transfers between devices: 354 us -> none  [reduce_items(): return lax.psum(term, 'item')]
    pallas_call x0 -> x1, Pallas kernels: none -> 127 us  [shards(): pl.pallas_call(kernel, out_shape=jax.ShapeDtypeStruct((SH, T), F32), in_s...]
    dot_general x4 -> x0, matrix products: 80.6 us -> none  [spread(): jnp.einsum('rsui,rsik->ruk', mixed, tiles_items, preferred_element_type=j...]
    psum x5 -> x0, blocking collectives: 70.9 us -> none  [the longest x3 42.7 us: norm_total(): return lax.psum(value, 'user')]
    reduce_sum x5 -> x0, other arithmetic: 17.6 us -> none  [the longest x3 9.57 us: shards(): alpha = norm_now / lax.psum(jnp.sum(direction * image), 'user')]
    all_to_all x1 -> x0, blocking collectives: 15.2 us -> none  [shards(): lax.all_to_all(mine.astype(jnp.bfloat16), ('user', 'item'), split_axis=0,...]
    convert_element_type x6 -> x0, other arithmetic: 14.2 us -> none  [the longest x3 10.8 us: shards(): rows = direction.astype(jnp.bfloat16)]
    gather x1 -> x0, local copies, waits for them, and re-layouts: 11.3 us -> none  [shards(): jnp.take(item_factors.reshape(col_tiles, tile, width), tile_cols, axis=0)]
  transfers between devices with their start and end apart: 4 -> 0, of which waited for: 4 -> 0; matrix products, arithmetic and copies ran while one was open for 0% -> 0% of each run, Pallas kernels for 0% -> 0%
where the time goes in v1:
time: 131 us; the launch traced here: 130 us
  Pallas kernels  127 us (97%)
  local copies, waits for them, and re-layouts  2.95 us (2%)
    pallas_call x1, Pallas kernels, shards(): pl.pallas_call(kernel, out_shape=jax.ShapeDtypeStruct((SH, T), F32), in_s...  127 us
    unnamed x2, local copies, waits for them, and re-layouts  2.95 us

profile of v1, /device:TPU:1, one launch (start us, length us, event | category | flops | bytes accessed | tf_op | source)
XLA Modules:
  0.0 129.7 jit_solution(4488420242586900195)
XLA Ops:
  0.0 1.4 %copy.6.cols = s32[32,12]{1,0:T(8,128)} copy(s32[32,12]{0,1:T(8,128)} %param.7) | data formatting | bytes 3072 | tf_op args[2]
  1.4 126.8 %shard_map.55 = f32[256,128]{1,0:T(8,128)} custom-call(s32[32,12]{1,0:T(8,128)} %copy.6.cols, bf16[32,12,128,128]{3,2,1,0:T(8,128)(2,1)} %w_hbm.1, bf16[32,12,128,128]{3,2,1,0:T(8,128)(2,1)} %r_hbm.1, bf16[32,128,128]{2,1,0:T(8,128)(2,1)} %bitcast.1, f32[4096,128]{1,0:T(8,128)} %x_hbm.1), custom_call_target="tpu_custom_call" | custom-call | tf_op jit(solution)/shard_map/pallas_call | solution.py:396
  128.2 1.6 %copy.8 = f32[256,128]{1,0:T(8,128)} copy(f32[256,128]{1,0:T(8,128)} %shard_map.55) | data formatting | bytes 262144

commit v2 on v1

--- a/solution.py
+++ b/solution.py
@@ -34,17 +34,28 @@
 
 
 def kernel(
-    cols, w_hbm, r_hbm, i_hbm, x_hbm, out,
-    w, rt, it, tt, x0, q0, q1, part, got, vec, wide, v0, y0, t1, y1, t2, acc, sj, og,
-    us_in, us_out, ps_in, ps_out, xd_out, xd_in,
-    w_sem, r_sem, i_sem, rs_s, rs_r, ag_s, ag_r, us_s, us_r, ps_s, ps_r, xd_s, xd_r,
+    c_hbm, w_hbm, r_hbm, i_hbm, x_hbm, out,
+    w, rt, it, tt, x0, q0, q1, part, got, part2, got2, vec, wide, v0, y0, t1, y1, t2, sj, og,
+    us_in, us_out, ps_in, ps_out, xd_out, xd_in, cols,
+    w_sem, r_sem, i_sem, rs_s, rs_r, r2_s, r2_r, ag_s, ag_r, fw_s, fw_r, us_s, us_r, ps_s, ps_r, xd_s, xd_r,
 ):
     u = lax.axis_index("user")
     i = lax.axis_index("item")
     x, z = i // 4, lax.rem(i, 4)
 
+    def at_offset(dx, dz):
+        return lax.rem(x + dx, 4) * 4 + lax.rem(z + dz, 4)
+
     def shard(k):
-        return lax.rem(x + near(k // 4), 4) * 4 + lax.rem(z + near(lax.rem(k, 4)), 4)
+        odd = lax.rem(k, 2)
+        m = k - 7
+        off = (k + 9) // 16
+        dx = (1 - off) * odd * near((k + 1) // 2) + off * near(1 + m // 3)
+        dz = (1 - off) * (1 - odd) * near(k // 2) + off * near(1 + lax.rem(m + 9, 3))
+        return at_offset(dx, dz)
+
+    def line_mate(axis, a):
+        return at_offset(near(a), 0) if axis == 0 else at_offset(0, near(a))
 
     def mate(k):
         return lax.rem(u + k, NU)
@@ -60,6 +71,7 @@
         return c
 
     load_i = pltpu.make_async_copy(i_hbm, it, i_sem.at[0])
+    load_c = pltpu.make_async_copy(c_hbm, cols, i_sem.at[2])
     load_x = pltpu.make_async_copy(x_hbm, x0, i_sem.at[1])
 
     def load_w(j):
@@ -70,6 +82,7 @@
         rows = pl.ds(2 * j, 2)
         return pltpu.make_async_copy(r_hbm.at[rows], rt.at[rows], r_sem.at[j])
 
+    load_c.start()
     load_i.start()
     load_x.start()
 
@@ -91,16 +104,52 @@
 
     lax.fori_loop(0, 32, turn, 0)
     load_x.wait()
-
-    def rs_copy(n, j):
-        return pltpu.make_async_remote_copy(
-            src_ref=part.at[n, j], dst_ref=got.at[n, i], send_sem=rs_s.at[n, j], recv_sem=rs_r.at[n, i],
-            device_id=(u, j), device_id_type=MESH)
-
-    def rs_arrival(n, j):
-        return pltpu.make_async_remote_copy(
-            src_ref=part.at[n, j], dst_ref=got.at[n, j], send_sem=rs_s.at[n, j], recv_sem=rs_r.at[n, j],
-            device_id=(u, j), device_id_type=MESH)
+    load_c.wait()
+
+    me = (x, z)
+
+    def place(axis, line):
+        return line * 4 + z if axis == 0 else x * 4 + line
+
+    def rs_copy(n, h, j):
+        jj = (j // 4, lax.rem(j, 4))
+        return pltpu.make_async_remote_copy(
+            src_ref=part.at[n, j, h * T:(h + 1) * T], dst_ref=got.at[n, h, me[1 - h], jj[h]], send_sem=rs_s.at[n, j, h],
+            recv_sem=rs_r.at[n, h, me[1 - h], jj[h]], device_id=(u, place(1 - h, jj[1 - h])), device_id_type=MESH)
+
+    def rs_arrival(n, h, line, group):
+        return pltpu.make_async_remote_copy(
+            src_ref=part.at[n, 0, 0:T], dst_ref=got.at[n, h, line, group], send_sem=rs_s.at[n, 0, h],
+            recv_sem=rs_r.at[n, h, line, group], device_id=(u, place(1 - h, line)), device_id_type=MESH)
+
+    def r2_copy(n, h, line, slot):
+        return pltpu.make_async_remote_copy(
+            src_ref=part2.at[n, h, line], dst_ref=got2.at[n, h, slot], send_sem=r2_s.at[n, h, line],
+            recv_sem=r2_r.at[n, h, slot], device_id=(u, place(h, line)), device_id_type=MESH)
+
+    def rs_send(n, j):
+        @pl.when(lax.rem(j, 4) != z)
+        def _():
+            rs_copy(n, 0, j).start()
+
+        @pl.when(j // 4 != x)
+        def _():
+            rs_copy(n, 1, j).start()
+
+    def line_sum(n, h, group):
+        total_ = part[n, place(h, group), h * T:(h + 1) * T, :].astype(F32)
+        for a in range(1, 4):
+            line = lax.rem(me[1 - h] + near(a), 4)
+            rs_arrival(n, h, line, group).wait_recv()
+            total_ += got[n, h, line, group].astype(F32)
+        return total_
+
+    def pass_on(n):
+        for a in range(1, 4):
+            for h in range(2):
+                line = lax.rem(me[h] + near(a), 4)
+                part2[n, h, line] = line_sum(n, h, line).astype(BF)
+                r2_copy(n, h, line, me[h]).start()
 
     def ag_copy(n, j):
         return pltpu.make_async_remote_copy(
@@ -111,6 +160,36 @@
         return pltpu.make_async_remote_copy(
             src_ref=vec.at[n, i], dst_ref=vec.at[n, j], send_sem=ag_s.at[n, j], recv_sem=ag_r.at[n, j],
             device_id=(u, j), device_id_type=MESH)
+
+    def half(axis):
+        return pl.ds(axis * T, T)
+
+    def fw_copy(n, j, k, axis, a):
+        rows = half(axis)
+        return pltpu.make_async_remote_copy(
+            src_ref=vec.at[n, j, rows], dst_ref=vec.at[n, j, rows], send_sem=fw_s.at[n, k, a - 1],
+            recv_sem=fw_r.at[n, j, axis], device_id=(u, line_mate(1 - axis, a)), device_id_type=MESH)
+
+    def line_in(n, k, axis):
+        j = shard(k)
+        ag_arrival(n, j).wait_recv()
+        for a in range(1, 4):
+            fw_copy(n, j, k, axis, a).start()
+
+    def lines_in(n, m):
+        line_in(n, 2 * m - 1, 0)
+        line_in(n, 2 * m, 1)
+
+    def vec_ready(n, k):
+        @pl.when(k <= 3)
+        def _():
+            lines_in(n, k)
+
+        @pl.when(k >= 7)
+        def _():
+            j = shard(k)
+            for axis in range(2):
+                fw_copy(n, j, 0, axis, 1).wait_recv()
 
     def us_copy(m, o, slot):
         return pltpu.make_async_remote_copy(
@@ -176,7 +255,7 @@
                 load_w(j).wait()
                 load_r(j).wait()
             else:
-                ag_arrival(n - 1, j).wait_recv()
+                vec_ready(n - 1, k)
 
         if first:
             ready(0)
@@ -191,15 +270,16 @@
                 @pl.when(kk == 0)
                 def _():
                     pl.semaphore_wait(bar, NI - 1 + NU - 1)
-                rs_copy(n, a).start()
-            else:
-                @pl.when(kk > 0)
-                def _():
-                    rs_copy(n, a).start()
+            rs_send(n, a)
             ready(2 * kk + 2)
             spread(n, b, q1)
             scores(n, at(2 * kk + 2), q0)
-            rs_copy(n, b).start()
+            rs_send(n, b)
+            if n == 2:
+                @pl.when(kk == 4)
+                def _():
+                    us_out[0] = plane_sum(0)
+                    user_send(0)
             return c
 
         lax.fori_loop(0, 7, two, 0)
@@ -207,25 +287,29 @@
         ready(15)
         spread(n, a, q0)
         scores(n, b, q1)
-        rs_copy(n, a).start()
-        spread(n, b, q1)
-        if not first:
-            rs_copy(n, b).start()
+        rs_send(n, a)
+        if first:
+            pass_on(n)
+            spread(n, b, q1)
+        else:
+            spread(n, b, q1)
+            rs_send(n, b)
+            pass_on(n)
 
     def collect(n):
-        acc[...] = part[n, i].astype(F32)
-
-        def add(k):
-            j = shard(k)
-            rs_arrival(n, j).wait_recv()
-            acc[...] += got[n, j].astype(F32)
-
-        each(1, NI, add)
-        return acc[...]
+        halves = []
+        for h in range(2):
+            sum_ = line_sum(n, h, me[h])
+            for a in range(1, 4):
+                line = lax.rem(me[h] + near(a), 4)
+                r2_copy(n, h, line, line).wait_recv()
+                sum_ += got2[n, h, line].astype(F32)
+            halves.append(sum_)
+        return jnp.concatenate(halves, axis=0)
 
     def publish(n, value):
         vec[n, i] = value.astype(BF)
-        each(1, NI, lambda k: ag_copy(n, shard(k)).start())
+        each(1, 7, lambda k: ag_copy(n, shard(k)).start())
 
     def user_send(m):
         each(1, NU, lambda k: us_copy(m, mate(k), u).start())
@@ -269,13 +353,11 @@
     alpha = div(total(vv), total(vy))
     t1[...] = v0[...] - alpha * y0[...]
     publish(1, t1[...])
-    us_out[0] = jnp.concatenate([vv, vy, zero, zero, zero, zero, zero, zero], axis=0)
-    user_send(0)
-
-    run_pass(2)
-    ps_out[0, 0:8, :] = user_sum(0)
+    ps_out[0, 0:8, :] = jnp.concatenate([vv, vy, zero, zero, zero, zero, zero, zero], axis=0)
     ps_out[0, 8:16, :] = jnp.zeros((8, T), F32)
     plane_send(0)
+
+    run_pass(2)
     y1[...] = collect(2) + RIDGE * t1[...]
     tt1 = lanes(t1[...] * t1[...])
     beta_own = div(total(tt1), total(vv))
@@ -290,17 +372,17 @@
     og[...] = jnp.concatenate([
         vy, ty0, ty1, lanes(t2[...] * y0[...]), lanes(t2[...] * y1[...]), lanes(t2[...] * t2[...]), zero, zero], axis=0)
 
-    sums0 = plane_sum(0)
+    sums0 = user_sum(0)
     rr0, vy_all = pick(sums0, 0), pick(sums0, 1)
     a0 = rr0 / vy_all
     rho = a0 * inv_alpha
     r1 = v0[...] - a0 * y0[...]
     z1 = rho * y1[...] + (1.0 - rho) * y0[...]
-    us_out[1] = jnp.concatenate([
+    ps_out[1, 0:8, :] = jnp.concatenate([
         lanes(r1 * r1), lanes(r1 * z1), lanes(r1 * y0[...]), lanes(v0[...] * z1), lanes(z1 * z1),
         lanes(z1 * y0[...]), lanes(y0[...] * y0[...]), zero], axis=0)
-    user_send(1)
     ps_out[1, 8:16, :] = jnp.concatenate([inv_alpha, inv_alpha1, beta_own, zero, zero, zero, zero, zero], axis=0)
+    plane_send(1)
 
     def squares(k):
         j = shard(k)
@@ -316,16 +398,16 @@
         sj[j] = out_sum
 
     def arrive_squares(k):
-        ag_arrival(2, shard(k)).wait_recv()
+        vec_ready(2, k)
         squares(k)
 
     squares(0)
-    each(1, 8, arrive_squares)
-    ps_out[1, 0:8, :] = user_sum(1)
-    plane_send(1)
-    each(8, NI, arrive_squares)
-
-    sums1 = plane_sum(1)
+    each(1, 10, arrive_squares)
+    us_out[1] = plane_sum(1)
+    user_send(1)
+    each(10, NI, arrive_squares)
+
+    sums1 = user_sum(1)
     rr1, r1z1, r1y0, v0z1, z1z1, z1y0, y0y0 = [pick(sums1, m) for m in range(7)]
     b0 = rr1 / rr0
     a1 = rr1 / (r1z1 + b0 * (r1y0 + v0z1) + b0 * b0 * vy_all)
@@ -375,9 +457,25 @@
     def sent_plane(k):
         j = shard(k)
         for n in range(3):
-            rs_copy(n, j).wait_send()
-            ag_copy(n, j).wait_send()
+            @pl.when(lax.rem(j, 4) != z)
+            def _():
+                rs_copy(n, 0, j).wait_send()
+
+            @pl.when(j // 4 != x)
+            def _():
+                rs_copy(n, 1, j).wait_send()
+
             ps_copy(n, j, i).wait_send()
+
+    def sent_lines(m):
+        for n in range(3):
+            for axis in range(2):
+                k = 2 * m - 1 + axis
+                j = shard(k)
+                ag_copy(n, j).wait_send()
+                r2_copy(n, axis, lax.rem(me[axis] + near(m), 4), me[axis]).wait_send()
+                for a in range(1, 4):
+                    fw_copy(n, j, k, axis, a).wait_send()
 
     def sent_user(k):
         o = mate(k)
@@ -386,6 +484,7 @@
         xd_copy(o, u).wait_send()
 
     each(1, NI, sent_plane)
+    each(1, 4, sent_lines)
     each(1, NU, sent_user)
 
 
@@ -396,19 +495,21 @@
     return pl.pallas_call(
         kernel,
         out_shape=jax.ShapeDtypeStruct((SH, T), F32),
-        in_specs=[pl.BlockSpec(memory_space=pltpu.SMEM), any_space, any_space, any_space, any_space],
+        in_specs=[any_space, any_space, any_space, any_space, any_space],
         out_specs=pl.BlockSpec(memory_space=vmem),
         scratch_shapes=[
             vmem((32, SLOTS, T, T), BF), vmem((32, SLOTS, T, T), BF),
             vmem((32, T, T), BF), vmem((32, T, T), BF), vmem((4096, T), F32),
             vmem((SH, SLOTS * T), BF), vmem((SH, SLOTS * T), BF),
-            vmem((3, NI, SH, T), BF), vmem((3, NI, SH, T), BF), vmem((3, NI, SH, T), BF), vmem((3, 4096, T), F32),
-            vmem((SH, T), F32), vmem((SH, T), F32), vmem((SH, T), F32), vmem((SH, T), F32), vmem((SH, T), F32), vmem((SH, T), F32),
+            vmem((3, NI, SH, T), BF), vmem((3, 2, 4, 4, T, T), BF), vmem((3, 2, 4, T, T), BF), vmem((3, 2, 4, T, T), BF),
+            vmem((3, NI, SH, T), BF), vmem((3, 4096, T), F32),
+            vmem((SH, T), F32), vmem((SH, T), F32), vmem((SH, T), F32), vmem((SH, T), F32), vmem((SH, T), F32),
             vmem((NI, 8, T), F32), vmem((8, T), F32),
             vmem((3, NU, 8, T), F32), vmem((3, 8, T), F32), vmem((3, NI, 16, T), F32), vmem((3, 16, T), F32),
             vmem((NU * 64, T), F32), vmem((NU, 64, T), F32),
-            dma((NI,)), dma((NI,)), dma((2,)),
-            dma((3, NI)), dma((3, NI)), dma((3, NI)), dma((3, NI)),
+            pltpu.SMEM((32, SLOTS), jnp.int32),
+            dma((NI,)), dma((NI,)), dma((3,)),
+            dma((3, NI, 2)), dma((3, 2, 4, 4)), dma((3, 2, 4)), dma((3, 2, 4)), dma((3, NI)), dma((3, NI)), dma((3, 7, 3)), dma((3, NI, 2)),
             dma((3, NU)), dma((3, NU)), dma((3, NI)), dma((3, NI)), dma((NU,)), dma((NU,)),
         ],
         compiler_params=pltpu.CompilerParams(

time: 131 us -> 111 us (0.85)
  Pallas kernels: 127 us -> 108 us
    pallas_call x1, Pallas kernels: 127 us -> 108 us  [shards(): pl.pallas_call(kernel, out_shape=jax.ShapeDtypeStruct((SH, T), F32), in_s...]
where the time goes in v2:
time: 111 us
  Pallas kernels  108 us (97%)
  local copies, waits for them, and re-layouts  2.95 us (3%)
    pallas_call x1, Pallas kernels, shards(): pl.pallas_call(kernel, out_shape=jax.ShapeDtypeStruct((SH, T), F32), in_s...  108 us
    unnamed x2, local copies, waits for them, and re-layouts  2.95 us

profile of v2, /device:TPU:1, one launch (start us, length us, event | category | flops | bytes accessed | tf_op | source)
XLA Modules:
  0.0 110.8 jit_solution(17640671214712078277)
XLA Ops:
  0.0 1.4 %copy.6.c_hbm = s32[32,12]{1,0:T(8,128)} copy(s32[32,12]{0,1:T(8,128)} %param.7) | data formatting | bytes 3072 | tf_op args[2]
  1.4 107.9 %shard_map.55 = f32[256,128]{1,0:T(8,128)} custom-call(s32[32,12]{1,0:T(8,128)} %copy.6.c_hbm, bf16[32,12,128,128]{3,2,1,0:T(8,128)(2,1)} %w_hbm.1, bf16[32,12,128,128]{3,2,1,0:T(8,128)(2,1)} %r_hbm.1, bf16[32,128,128]{2,1,0:T(8,128)(2,1)} %bitcast.1, f32[4096,128]{1,0:T(8,128)} %x_hbm.1), custom_call_target="tpu_custom_call" | custom-call | tf_op jit(solution)/shard_map/pallas_call | solution.py:495
  109.2 1.6 %copy.8 = f32[256,128]{1,0:T(8,128)} copy(f32[256,128]{1,0:T(8,128)} %shard_map.55) | data formatting | bytes 262144

commit v3 on v2

--- a/solution.py
+++ b/solution.py
@@ -16,8 +16,12 @@
 SH = 256
 
 
+def quo(a, b):
+    return a // b if isinstance(a, int) else lax.div(a, jnp.int32(b))
+
+
 def near(a):
-    return a + a // 2 - 2 * (a // 3)
+    return a + quo(a, 2) - 2 * quo(a + 1, 4)
 
 
 def div(a, b):
@@ -35,7 +39,7 @@
 
 def kernel(
     c_hbm, w_hbm, r_hbm, i_hbm, x_hbm, out,
-    w, rt, it, tt, x0, q0, q1, part, got, part2, got2, vec, wide, v0, y0, t1, y1, t2, sj, og,
+    w, rt, it, x0, q0, q1, part, got, part2, got2, vec, wide, v0, y0, t1, y1, t2, sj, og,
     us_in, us_out, ps_in, ps_out, xd_out, xd_in, cols,
     w_sem, r_sem, i_sem, rs_s, rs_r, r2_s, r2_r, ag_s, ag_r, fw_s, fw_r, us_s, us_r, ps_s, ps_r, xd_s, xd_r,
 ):
@@ -47,11 +51,13 @@
         return lax.rem(x + dx, 4) * 4 + lax.rem(z + dz, 4)
 
     def shard(k):
-        odd = lax.rem(k, 2)
-        m = k - 7
-        off = (k + 9) // 16
-        dx = (1 - off) * odd * near((k + 1) // 2) + off * near(1 + m // 3)
-        dz = (1 - off) * (1 - odd) * near(k // 2) + off * near(1 + lax.rem(m + 9, 3))
+        if isinstance(k, int):
+            off, odd, m = k // 7 if k < 14 else 1, k % 2, max(k - 7, 0)
+        else:
+            off, odd, m = quo(k + 9, 16), lax.rem(k, 2), k - 7
+        third = quo(m * 11, 32)
+        dx = (1 - off) * odd * near(quo(k + 1, 2)) + off * near(1 + third)
+        dz = (1 - off) * (1 - odd) * near(quo(k, 2)) + off * near(1 + m - 3 * third)
         return at_offset(dx, dz)
 
     def line_mate(axis, a):
@@ -98,11 +104,6 @@
 
     load_i.wait()
 
-    def turn(c, carry):
-        tt[c] = it[c].T
-        return carry
-
-    lax.fori_loop(0, 32, turn, 0)
     load_x.wait()
     load_c.wait()
 
@@ -213,8 +214,8 @@
         lax.fori_loop(lo, hi, body, 0)
 
     def score_pair(d, r, p):
-        t = jnp.concatenate([tt[cols[r, 2 * p]], tt[cols[r, 2 * p + 1]]], axis=1)
-        return jnp.dot(d, t, preferred_element_type=F32)
+        t = jnp.concatenate([it[cols[2 * p, r]], it[cols[2 * p + 1, r]]], axis=0)
+        return lax.dot_general(d, t, (((1,), (1,)), ((), ())), preferred_element_type=F32)
 
     def weight_pair(ref, r, p):
         return jnp.concatenate([ref[r, 2 * p], ref[r, 2 * p + 1]], axis=1).astype(F32)
@@ -239,7 +240,7 @@
     def spread(n, j, q):
         for h in range(2):
             r = 2 * j + h
-            items = jnp.concatenate([it[cols[r, b]] for b in range(SLOTS)], axis=0)
+            items = jnp.concatenate([it[cols[b, r]] for b in range(SLOTS)], axis=0)
             part[n, j, h * T:(h + 1) * T, :] = jnp.dot(
                 q[h * T:(h + 1) * T, :], items, preferred_element_type=F32).astype(BF)
 
@@ -267,14 +268,26 @@
             spread(n, a, q0)
             scores(n, b, q1)
             if first:
-                @pl.when(kk == 0)
+                @pl.when(kk == 2)
                 def _():
                     pl.semaphore_wait(bar, NI - 1 + NU - 1)
-            rs_send(n, a)
+                    for k in range(4):
+                        rs_send(n, at(k))
+
+                @pl.when(kk >= 2)
+                def _():
+                    rs_send(n, a)
+            else:
+                rs_send(n, a)
             ready(2 * kk + 2)
             spread(n, b, q1)
             scores(n, at(2 * kk + 2), q0)
-            rs_send(n, b)
+            if first:
+                @pl.when(kk >= 2)
+                def _():
+                    rs_send(n, b)
+            else:
+                rs_send(n, b)
             if n == 2:
                 @pl.when(kk == 4)
                 def _():
@@ -402,10 +415,10 @@
         squares(k)
 
     squares(0)
-    each(1, 10, arrive_squares)
+    each(1, 5, arrive_squares)
     us_out[1] = plane_sum(1)
     user_send(1)
-    each(10, NI, arrive_squares)
+    each(5, NI, arrive_squares)
 
     sums1 = user_sum(1)
     rr1, r1z1, r1y0, v0z1, z1z1, z1y0, y0y0 = [pick(sums1, m) for m in range(7)]
@@ -450,10 +463,6 @@
     plane_send(2)
     xd_in[u] = xd_out[pl.ds(pl.multiple_of(u * 64, 64), 64), :]
     each(1, NU, lambda k: xd_copy(mate(k), mate(k)).wait_recv())
-    a2 = rr2 / pick(plane_sum(2), 0)
-    for o in range(NU):
-        out[o * 32:(o + 1) * 32, :] = xd_in[o, 0:32, :] + a2 * xd_in[o, 32:64, :]
-
     def sent_plane(k):
         j = shard(k)
         for n in range(3):
@@ -465,7 +474,8 @@
             def _():
                 rs_copy(n, 1, j).wait_send()
 
-            ps_copy(n, j, i).wait_send()
+            if n < 2:
+                ps_copy(n, j, i).wait_send()
 
     def sent_lines(m):
         for n in range(3):
@@ -486,6 +496,11 @@
     each(1, NI, sent_plane)
     each(1, 4, sent_lines)
     each(1, NU, sent_user)
+
+    a2 = rr2 / pick(plane_sum(2), 0)
+    for o in range(NU):
+        out[o * 32:(o + 1) * 32, :] = xd_in[o, 0:32, :] + a2 * xd_in[o, 32:64, :]
+    each(1, NI, lambda k: ps_copy(2, shard(k), i).wait_send())
 
 
 def shards(weights, ratings, tile_cols, item_factors, old_users):
@@ -499,7 +514,7 @@
         out_specs=pl.BlockSpec(memory_space=vmem),
         scratch_shapes=[
             vmem((32, SLOTS, T, T), BF), vmem((32, SLOTS, T, T), BF),
-            vmem((32, T, T), BF), vmem((32, T, T), BF), vmem((4096, T), F32),
+            vmem((32, T, T), BF), vmem((4096, T), F32),
             vmem((SH, SLOTS * T), BF), vmem((SH, SLOTS * T), BF),
             vmem((3, NI, SH, T), BF), vmem((3, 2, 4, 4, T, T), BF), vmem((3, 2, 4, T, T), BF), vmem((3, 2, 4, T, T), BF),
             vmem((3, NI, SH, T), BF), vmem((3, 4096, T), F32),
@@ -507,14 +522,14 @@
             vmem((NI, 8, T), F32), vmem((8, T), F32),
             vmem((3, NU, 8, T), F32), vmem((3, 8, T), F32), vmem((3, NI, 16, T), F32), vmem((3, 16, T), F32),
             vmem((NU * 64, T), F32), vmem((NU, 64, T), F32),
-            pltpu.SMEM((32, SLOTS), jnp.int32),
+            pltpu.SMEM((SLOTS, 32), jnp.int32),
             dma((NI,)), dma((NI,)), dma((3,)),
             dma((3, NI, 2)), dma((3, 2, 4, 4)), dma((3, 2, 4)), dma((3, 2, 4)), dma((3, NI)), dma((3, NI)), dma((3, 7, 3)), dma((3, NI, 2)),
             dma((3, NU)), dma((3, NU)), dma((3, NI)), dma((3, NI)), dma((NU,)), dma((NU,)),
         ],
         compiler_params=pltpu.CompilerParams(
             collective_id=0, has_side_effects=True, vmem_limit_bytes=56 * 2 ** 20),
-    )(tile_cols, weights, ratings, item_factors.reshape(32, T, T), old_users)
+    )(tile_cols.T, weights, ratings, item_factors.reshape(32, T, T), old_users)
 
 
 def solution(mesh):

time: 111 us -> 102 us (0.919)
  Pallas kernels: 108 us -> 100 us
  local copies, waits for them, and re-layouts: 2.95 us -> 1.57 us
    pallas_call x1, Pallas kernels: 108 us -> 100 us  [shards(): pl.pallas_call(kernel, out_shape=jax.ShapeDtypeStruct((SH, T), F32), in_s...]
    unnamed x2 -> x1, local copies, waits for them, and re-layouts: 2.95 us -> 1.57 us
where the time goes in v3:
time: 102 us
  Pallas kernels  100 us (98%)
  local copies, waits for them, and re-layouts  1.57 us (2%)
    pallas_call x1, Pallas kernels, shards(): pl.pallas_call(kernel, out_shape=jax.ShapeDtypeStruct((SH, T), F32), in_s...  100 us

profile of v3, /device:TPU:1, one launch (start us, length us, event | category | flops | bytes accessed | tf_op | source)
XLA Modules:
  0.0 101.6 jit_solution(1824394953032311586)
XLA Ops:
  0.0 100.0 %shard_map.55 = f32[256,128]{1,0:T(8,128)} custom-call(s32[12,32]{1,0:T(8,128)} %bitcast.3, bf16[32,12,128,128]{3,2,1,0:T(8,128)(2,1)} %w_hbm.1, bf16[32,12,128,128]{3,2,1,0:T(8,128)(2,1)} %r_hbm.1, bf16[32,128,128]{2,1,0:T(8,128)(2,1)} %bitcast.2, f32[4096,128]{1,0:T(8,128)} %x_hbm.1), custom_call_target="tpu_custom_call" | custom-call | tf_op jit(solution)/shard_map/pallas_call | solution.py:510
  100.0 1.6 %copy.7 = f32[256,128]{1,0:T(8,128)} copy(f32[256,128]{1,0:T(8,128)} %shard_map.55) | data formatting | bytes 262144
